TPU v7x, 128 devices: a whole 4x4x4 slice. The times are simulated.
128 devices in a mesh: row: 8 (over y, core), col: 16 (over z, x).
Axes of the slice: x: 4, y: 4, z: 4, core: 2. Of those that a mesh axis runs over, the one named last changes fastest.
Arguments:
- tokens: bfloat16 [256, 512, 1024], P('row', 'col'), may hold values from -6 to 6
- ln_gain: float32 [1024], replicated, may hold values from 0.25 to 1.75
- w_query: bfloat16 [1024, 1024], replicated, may hold values from -0.1875 to 0.1875
- w_keyval: bfloat16 [1024, 2048], replicated, may hold values from -0.1875 to 0.1875
- logit_scale: float32 [16], replicated, may hold values from 2 to 40
- w_output: bfloat16 [1024, 1024], replicated, may hold values from -0.75 to 0.75
- parents: int32 [32, 64, 3, 8], P('row', 'col'), may hold values from 0 to 32767, as said below
- child_counts: int32 [32, 64, 3, 8], P('row', 'col'), may hold values from 1 to 4
Outputs:
- mixed: bfloat16 [256, 512, 1024], P('row', 'col')
Inputs may be any that keep to these rules, and one draw needn't show every extreme that they name: `parents`: The 8 entries of one tile and level are distinct, and so are all entries of one level over the tiles of one device. Over the tiles of one device and one level at most 2 entries name cells in the block of one device, and in every draw some device receives exactly 2 from some device at every level.
All inputs are finite; a program needn't handle non-finite values.
Results may differ from a plain program's by a relative error of at most 0.012.
The roundings to bfloat16 on the way count: a program that leaves them out, or rounds other values in their place, can miss the bound.
Values may be sent and summed in bfloat16 or wider, within the bound.
A program may use at most 128 MiB of HBM per device.

v0:
```python
import functools

import jax
import jax.numpy as jnp
from jax import lax
from jax.experimental import pallas as pl
from jax.experimental.pallas import tpu as pltpu
from jax.sharding import PartitionSpec as P

TILE = 8
LEVELS = 3
TOPK = 8
EPSILON = 1e-06
F32 = jnp.float32
BF16 = jnp.bfloat16
MESH = pl.DeviceIdType.MESH

DEVICES = 128
N_COL = 16
SIDE = 32
TOKENS = SIDE * SIDE
TILES = 16
REQUESTS = TILES * TOPK
WIDTH = 1024
HALF = WIDTH // 2
HEAD = 64
GROUP = 256
OWN = TILE * TILE
PER_LEVEL = TOPK * 4
KEYS = OWN + LEVELS * PER_LEVEL
STEP = 37
SERVED = 32


def shifted(place, sign):
    offset = lax.rem(place * STEP, DEVICES)
    row, col = lax.axis_index("row"), lax.axis_index("col")
    core = lax.rem(lax.rem(row, 2) + lax.rem(offset, 2), 2)
    x = lax.rem(lax.rem(col, 4) + sign * lax.rem(offset // 2, 4) + 4, 4)
    z = lax.rem(col // 4 + sign * lax.rem(offset // 8, 4) + 4, 4)
    y = lax.rem(row // 2 + sign * (offset // 32) + 4, 4)
    return y * 2 + core, z * 4 + x


def iota(shape, axis):
    return lax.broadcasted_iota(jnp.int32, shape, axis)


def ones_where(condition):
    return jnp.where(condition, 1.0, 0.0)


def dot(a, b):
    return jnp.dot(a, b, preferred_element_type=F32)


def same_head():
    return ones_where(iota((GROUP, GROUP), 0) // HEAD == iota((GROUP, GROUP), 1) // HEAD).astype(BF16)


def unit_heads(values, block_ones):
    squares = values * values
    high = squares.astype(BF16)
    low = (squares - high.astype(F32)).astype(BF16)
    total = dot(high, block_ones) + dot(low, block_ones)
    return values * lax.rsqrt(total + EPSILON)


def column_of(raw_ref, level):
    raw = raw_ref[...].reshape(TILES, LEVELS, TOPK)[:, level : level + 1, :].astype(F32)
    spread = jnp.broadcast_to(raw, (TILES, TOPK, TOPK))
    keep = iota((TILES, TOPK, TOPK), 1) == iota((TILES, TOPK, TOPK), 2)
    return jnp.sum(jnp.where(keep, spread, 0.0), axis=2, keepdims=True).reshape(REQUESTS, 1)


def row_of(column):
    square = (REQUESTS, REQUESTS)
    spread = jnp.broadcast_to(column, square)
    return jnp.sum(jnp.where(iota(square, 0) == iota(square, 1), spread, 0.0), axis=0, keepdims=True)


def kernel(
    tokens_hbm, gain_ref, w_query_hbm, w_keyval_hbm, scale_ref, w_output_hbm, parents_ref, counts_ref,
    out_ref,
    tokens, w_query, w_keyval, w_output, normed, queries, keys, values, marks, attended, picked,
    ask, asked, send, recv, place_of,
    load_sem, ask_send, ask_recv, reply_send, reply_recv, self_sem,
):
    square = (REQUESTS, REQUESTS)
    loads = [
        pltpu.make_async_copy(source, target, load_sem.at[number])
        for number, (source, target) in enumerate(
            ((tokens_hbm, tokens), (w_keyval_hbm, w_keyval), (w_query_hbm, w_query), (w_output_hbm, w_output))
        )
    ]
    for load in loads:
        load.start()

    barrier = pltpu.get_barrier_semaphore()

    def greet(place, carry):
        pl.semaphore_signal(barrier, inc=1, device_id=shifted(place, 1), device_id_type=MESH)
        return carry

    lax.fori_loop(1, DEVICES, greet, 0)

    lane = iota(square, 1)
    lane_level, lane_slot, lane_child = lane // 8, lane // 4 % 2, lane % 4
    table = jnp.zeros(square, F32)
    for level in range(LEVELS):
        parent_col = column_of(parents_ref, level).astype(jnp.int32)
        parent_row = row_of(parent_col.astype(F32)).astype(jnp.int32)
        bits = 8 - 2 * level
        home_col, home_row = parent_col >> bits, parent_row >> bits
        local_row = (parent_row & ((1 << bits) - 1)).astype(F32)
        same = home_col == home_row
        rank_col = jnp.sum(ones_where(same & (iota(square, 1) < iota(square, 0))), axis=1, keepdims=True)
        rank_row = jnp.sum(ones_where(same & (iota(square, 0) < iota(square, 1))), axis=0, keepdims=True)
        place_of[level] = jnp.broadcast_to(home_col * 8 + rank_col.astype(jnp.int32) * 4, square)
        for slot in range(2):
            here = (iota(square, 0) == home_row) & (rank_row == float(slot))
            cell = jnp.sum(jnp.where(here, local_row, 0.0), axis=1, keepdims=True)
            table = jnp.where((lane_level == level) & (lane_slot == slot), cell, table)
    local = table.astype(jnp.int32)
    wide_bits = 4 - lane_level
    parent_r, parent_c = local >> wide_bits, local & ((1 << wide_bits) - 1)
    child = ((2 * parent_r + lane_child // 2) << (wide_bits + 1)) + 2 * parent_c + lane_child % 2
    ask[...] = child.reshape(DEVICES, 1, REQUESTS)

    me = lax.axis_index("row") * N_COL + lax.axis_index("col")
    own_ask = pltpu.make_async_copy(ask.at[me], asked.at[0], self_sem.at[LEVELS])
    own_ask.start()
    pl.semaphore_wait(barrier, DEVICES - 1)

    def send_ask(place, carry):
        row, col = shifted(place, -1)
        pltpu.make_async_remote_copy(
            src_ref=ask.at[row * N_COL + col], dst_ref=asked.at[place], send_sem=ask_send, recv_sem=ask_recv,
            device_id=(row, col), device_id_type=MESH,
        ).start()
        return carry

    lax.fori_loop(1, DEVICES, send_ask, 0)

    loads[0].wait()
    gain = gain_ref[...].reshape(1, WIDTH)

    def norm_rows(pair, carry):
        flat = tokens[pl.ds(2 * pair, 2)].reshape(2 * SIDE, WIDTH).astype(F32)
        centered = flat - jnp.mean(flat, axis=1, keepdims=True)
        spread = jnp.mean(centered * centered, axis=1, keepdims=True)
        result = centered * lax.rsqrt(spread + EPSILON) * gain
        tiled = result.reshape(2, 4, TILE, WIDTH).transpose(1, 0, 2, 3).reshape(4, 16, WIDTH).astype(BF16)
        for tile in range(4):
            start = pl.multiple_of((pair // 4 * 4 + tile) * OWN + pair % 4 * 16, 16)
            normed[pl.ds(start, 16), :] = tiled[tile]
        return carry

    lax.fori_loop(0, SIDE // 2, norm_rows, 0)

    own_ask.wait()
    pltpu.make_async_remote_copy(
        src_ref=ask.at[pl.ds(0, DEVICES - 1)], dst_ref=asked.at[pl.ds(0, DEVICES - 1)], send_sem=ask_send,
        recv_sem=ask_recv, device_id=shifted(1, 1), device_id_type=MESH,
    ).wait()
    token = iota((1, TOKENS), 1)
    token_r = token // 256 * 8 + token // 8 % 8
    token_c = token // 64 % 4 * 8 + token % 8
    place_in_eight = iota((SERVED, 8, REQUESTS), 1)
    lane_in_eight = iota((SERVED, 8, REQUESTS), 2)
    for level in range(LEVELS):
        cell_of = (token_r >> level) * (SIDE >> level) + (token_c >> level)

        def serve(block, carry):
            first = pl.multiple_of(block * SERVED, SERVED)
            wanted = jnp.broadcast_to(asked[pl.ds(first, SERVED)].astype(F32), (SERVED, 8, REQUESTS))
            wanted = jnp.where(lane_in_eight == place_in_eight + 8 * level, wanted, 0.0)
            wanted = jnp.sum(wanted, axis=2, keepdims=True).reshape(SERVED * 8, 1).astype(jnp.int32)
            pick = jnp.where(wanted == cell_of, 0.25**level, 0.0).astype(BF16)
            left = dot(pick, normed[:, :HALF]).reshape(SERVED, 8, HALF)
            right = dot(pick, normed[:, HALF:]).reshape(SERVED, 8, HALF)
            send[level, pl.ds(first, SERVED)] = jnp.concatenate([left, right], axis=1).astype(BF16)

            def send_reply(place, carry):
                row, col = shifted(place, 1)
                pltpu.make_async_remote_copy(
                    src_ref=send.at[level, place], dst_ref=recv.at[level, me], send_sem=reply_send.at[level],
                    recv_sem=reply_recv.at[level], device_id=(row, col), device_id_type=MESH,
                ).start()
                return carry

            lax.fori_loop(jnp.maximum(first, 1), first + SERVED, send_reply, 0)
            return carry

        lax.fori_loop(0, DEVICES // SERVED, serve, 0)
        pltpu.make_async_copy(send.at[level, 0], recv.at[level, me], self_sem.at[level]).start()

    block_ones = same_head()
    loads[1].wait()
    loads[2].wait()

    def project(block, carry):
        rows = pl.ds(pl.multiple_of(block * GROUP, GROUP), GROUP)
        tiles = pl.ds(block * 4, 4)
        flat = normed[rows, :]
        for group in range(WIDTH // GROUP):
            span = slice(group * GROUP, (group + 1) * GROUP)
            query = unit_heads(dot(flat, w_query[:, span]), block_ones) * scale_ref[:, span]
            queries[rows, span] = query.astype(BF16)
            key = dot(flat, w_keyval[:, span]).astype(BF16).astype(F32)
            keys[tiles, 0:OWN, span] = unit_heads(key, block_ones).astype(BF16).reshape(4, OWN, GROUP)
            value = dot(flat, w_keyval[:, WIDTH + group * GROUP : WIDTH + (group + 1) * GROUP])
            values[tiles, 0:OWN, span] = value.astype(BF16).reshape(4, OWN, GROUP)
        return carry

    lax.fori_loop(0, TOKENS // GROUP, project, 0)
    marks[:, 0:OWN, :] = jnp.ones((TILES, OWN, REQUESTS), BF16)

    def by_tile(rows):
        columns = rows.shape[-1]
        return rows.reshape(4, TILES, TOPK, columns).transpose(1, 0, 2, 3).reshape(TILES, PER_LEVEL, columns)

    slots = iota((REQUESTS, DEVICES * 8), 1)
    for level in range(LEVELS):
        pltpu.make_async_copy(send.at[level, 0], recv.at[level, me], self_sem.at[level]).wait()
        pltpu.make_async_remote_copy(
            src_ref=send.at[level, pl.ds(0, DEVICES - 1)], dst_ref=recv.at[level, pl.ds(0, DEVICES - 1)],
            send_sem=reply_send.at[level], recv_sem=reply_recv.at[level], device_id=shifted(1, 1),
            device_id_type=MESH,
        ).wait()
        count_col = column_of(counts_ref, level)
        place_col = place_of[level][:, 0:1]
        valid = [count_col > float(child) for child in range(4)]
        marks[:, OWN + level * PER_LEVEL : OWN + (level + 1) * PER_LEVEL, :] = by_tile(
            jnp.concatenate([jnp.broadcast_to(ones_where(flag), square) for flag in valid], axis=0)
        ).astype(BF16)
        for side in range(2):
            rows = recv[level].astype(F32)[:, side * 8 : side * 8 + 8, :].reshape(DEVICES * 8, HALF).astype(BF16)
            for child in range(4):
                pick = ones_where((slots == place_col + child) & valid[child]).astype(BF16)
                picked[child * REQUESTS : (child + 1) * REQUESTS, side * HALF : (side + 1) * HALF] = dot(
                    pick, rows
                ).astype(BF16)
        span_rows = slice(OWN + level * PER_LEVEL, OWN + (level + 1) * PER_LEVEL)
        for group in range(WIDTH // GROUP):
            span = slice(group * GROUP, (group + 1) * GROUP)
            key = dot(picked[...], w_keyval[:, span]).astype(BF16).astype(F32)
            keys[:, span_rows, span] = by_tile(unit_heads(key, block_ones)).astype(BF16)
            value = dot(picked[...], w_keyval[:, WIDTH + group * GROUP : WIDTH + (group + 1) * GROUP])
            values[:, span_rows, span] = by_tile(value).astype(BF16)

    loads[3].wait()
    head_of = iota((OWN, GROUP), 1) // HEAD

    def four_tiles(block, carry):
        def one_tile(tile, carry):
            rows = pl.ds(pl.multiple_of(tile * OWN, OWN), OWN)
            for group in range(WIDTH // GROUP):
                span = slice(group * GROUP, (group + 1) * GROUP)
                query = queries[rows, span].astype(F32)
                stacked = jnp.concatenate(
                    [jnp.where(head_of == head, query, 0.0).astype(BF16) for head in range(4)], axis=0
                )
                score = lax.dot_general(
                    stacked, keys[tile, :, span], (((1,), (1,)), ((), ())), preferred_element_type=F32
                )
                weight = jnp.exp(score).astype(BF16)
                total = dot(weight, marks[tile])
                total = jnp.concatenate([total, total], axis=1)
                mixed = dot(weight, values[tile, :, span])
                top, bottom = mixed[0:OWN], total[0:OWN]
                for head in range(1, 4):
                    top = jnp.where(head_of == head, mixed[head * OWN : (head + 1) * OWN], top)
                    bottom = jnp.where(head_of == head, total[head * OWN : (head + 1) * OWN], bottom)
                attended[rows, span] = (top / bottom).astype(BF16)
            return carry

        lax.fori_loop(block * 4, block * 4 + 4, one_tile, 0)
        flat = attended[pl.ds(pl.multiple_of(block * GROUP, GROUP), GROUP), :]
        for side in range(2):
            span = slice(side * HALF, (side + 1) * HALF)
            mixed = dot(flat, w_output[:, span]).reshape(4, TILE, TILE, HALF)
            mixed = mixed.transpose(1, 0, 2, 3).reshape(TILE, SIDE, HALF).astype(BF16)
            out_ref[pl.ds(block * TILE, TILE), :, span] = mixed
        return carry

    lax.fori_loop(0, TILES // 4, four_tiles, 0)


def per_device(tokens, ln_gain, w_query, w_keyval, logit_scale, w_output, parents, child_counts):
    scale_row = jnp.repeat(logit_scale, HEAD).reshape(1, WIDTH)
    whole = pl.BlockSpec(memory_space=pltpu.VMEM)
    anywhere = pl.BlockSpec(memory_space=pl.ANY)
    return pl.pallas_call(
        kernel,
        out_shape=jax.ShapeDtypeStruct((SIDE, SIDE, WIDTH), BF16),
        in_specs=[anywhere, whole, anywhere, anywhere, whole, anywhere, whole, whole],
        out_specs=whole,
        scratch_shapes=[
            pltpu.VMEM((SIDE, SIDE, WIDTH), BF16),
            pltpu.VMEM((WIDTH, WIDTH), BF16),
            pltpu.VMEM((WIDTH, 2 * WIDTH), BF16),
            pltpu.VMEM((WIDTH, WIDTH), BF16),
            pltpu.VMEM((TOKENS, WIDTH), BF16),
            pltpu.VMEM((TOKENS, WIDTH), BF16),
            pltpu.VMEM((TILES, KEYS, WIDTH), BF16),
            pltpu.VMEM((TILES, KEYS, WIDTH), BF16),
            pltpu.VMEM((TILES, KEYS, REQUESTS), BF16),
            pltpu.VMEM((TOKENS, WIDTH), BF16),
            pltpu.VMEM((4 * REQUESTS, WIDTH), BF16),
            pltpu.VMEM((DEVICES, 1, REQUESTS), jnp.int32),
            pltpu.VMEM((DEVICES, 1, REQUESTS), jnp.int32),
            pltpu.VMEM((LEVELS, DEVICES, 16, HALF), BF16),
            pltpu.VMEM((LEVELS, DEVICES, 16, HALF), BF16),
            pltpu.VMEM((LEVELS, REQUESTS, REQUESTS), jnp.int32),
            pltpu.SemaphoreType.DMA((4,)),
            pltpu.SemaphoreType.DMA,
            pltpu.SemaphoreType.DMA,
            pltpu.SemaphoreType.DMA((LEVELS,)),
            pltpu.SemaphoreType.DMA((LEVELS,)),
            pltpu.SemaphoreType.DMA((LEVELS + 1,)),
        ],
        compiler_params=pltpu.CompilerParams(
            collective_id=0, has_side_effects=True, vmem_limit_bytes=60 * 2**20
        ),
    )(tokens, ln_gain, w_query, w_keyval, scale_row, w_output, parents, child_counts)


def solution(mesh):
    in_specs = (
        P("row", "col", None),
        P(),
        P(),
        P(),
        P(),
        P(),
        P("row", "col", None, None),
        P("row", "col", None, None),
    )
    return jax.shard_map(
        per_device, mesh=mesh, in_specs=in_specs, out_specs=P("row", "col", None), check_vma=False
    )
```

profile of v0, /device:TPU:9, one launch (start us, length us, event | category | flops | bytes accessed | tf_op | source)
XLA Modules:
  0.0 127.6 jit_solution(3866398435190867669)
XLA Ops:
  0.0 0.7 broadcast_in_dim.3
  0.7 0.7 reshape_reshape.3.scale_ref
  1.4 1.4 %copy.9.parents_ref = s32[4,4,3,8]{3,2,1,0:T(4,128)} copy(s32[4,4,3,8]{3,1,2,0:T(4,128)} %param.14) | data formatting | bytes 3072 | tf_op args[6]
  2.8 1.3 %copy.10.counts_ref = s32[4,4,3,8]{3,2,1,0:T(4,128)} copy(s32[4,4,3,8]{3,1,2,0:T(4,128)} %param.15) | data formatting | bytes 3072 | tf_op args[7]
  4.1 120.3 %shard_map.82 = bf16[32,32,1024]{2,1,0:T(8,128)(2,1)} custom-call(bf16[32,32,1024]{2,1,0:T(8,128)(2,1)} %tokens_hbm.1, f32[1024]{0:T(1024)} %gain_ref.1, bf16[1024,1024]{1,0:T(8,128)(2,1)} %w_query_hbm.1, bf16[1024,2048]{1,0:T(8,128)(2,1)} %w_keyval_hbm.1, f32[1,1024]{1,0:T(1,128)} %reshape_reshape.3.scale_ref, bf16[1024,1024]{1,0:T(8,128)(2,1)} %w_output_hbm.1, ...), custom_call_target="tpu_custom_call" | custom-call | tf_op jit(solution)/shard_map/pallas_call | solution.py:294
  124.4 3.2 %copy.12 = bf16[32,32,1024]{2,1,0:T(8,128)(2,1)} copy(bf16[32,32,1024]{2,1,0:T(8,128)(2,1)} %shard_map.82) | data formatting | bytes 4194304
where the time goes:
time: 129 us; the launch traced here: 128 us
  Pallas kernels  120 us (93%)
  local copies, waits for them, and re-layouts  7.29 us (6%)
    pallas_call x1, Pallas kernels, per_device(): pl.pallas_call(kernel, out_shape=jax.ShapeDtypeStruct((SIDE, SIDE, WIDTH)...  120 us
    unnamed x3, local copies, waits for them, and re-layouts  5.89 us

commit v1 on v0

v1 whole, which is shorter than its diff:
```python
import functools

import jax
import jax.numpy as jnp
from jax import lax
from jax.experimental import pallas as pl
from jax.experimental.pallas import tpu as pltpu
from jax.sharding import PartitionSpec as P

TILE = 8
LEVELS = 3
TOPK = 8
EPSILON = 1e-06
F32 = jnp.float32
BF16 = jnp.bfloat16
MESH = pl.DeviceIdType.MESH

DEVICES = 128
N_COL = 16
SIDE = 32
TOKENS = SIDE * SIDE
TILES = 16
REQUESTS = TILES * TOPK
WIDTH = 1024
HALF = WIDTH // 2
HEAD = 64
GROUP = 256
OWN = TILE * TILE
PER_LEVEL = TOPK * 4
KEYS = OWN + LEVELS * PER_LEVEL
N_ROW = 8
SERVED = 32


def wrap(value):
    return jnp.where(value >= 4, value - 4, value)


def row_shifted(place):
    row = lax.axis_index("row")
    y, core = lax.div(row, 2), lax.rem(row, 2)
    return wrap(y + place // 2) * 2 + (1 - core if place % 2 else core)


def col_shifted(place, sign):
    col = lax.axis_index("col")
    off_z = place % 4
    off_x = (place // 4 + 3 * off_z) % 4
    z = wrap(lax.div(col, 4) + (sign * off_z) % 4)
    x = wrap(lax.rem(col, 4) + (sign * off_x) % 4)
    return z * 4 + x


def iota(shape, axis):
    return lax.broadcasted_iota(jnp.int32, shape, axis)


def ones_where(condition):
    return jnp.where(condition, 1.0, 0.0)


def dot(a, b):
    return jnp.dot(a, b, preferred_element_type=F32)


def dot_rows(a, b):
    return lax.dot_general(a, b, (((1,), (1,)), ((), ())), preferred_element_type=F32)


def same_head():
    return ones_where(iota((GROUP, GROUP), 0) // HEAD == iota((GROUP, GROUP), 1) // HEAD).astype(BF16)


def unit_heads(values, block_ones):
    squares = values * values
    high = squares.astype(BF16)
    low = (squares - high.astype(F32)).astype(BF16)
    total = dot(high, block_ones) + dot(low, block_ones)
    return values * lax.rsqrt(total + EPSILON)


def column_of(raw_ref, level):
    raw = raw_ref[:, level].astype(F32).reshape(TILES, 1, TOPK)
    spread = jnp.broadcast_to(raw, (TILES, TOPK, TOPK))
    keep = iota((TILES, TOPK, TOPK), 1) == iota((TILES, TOPK, TOPK), 2)
    return jnp.sum(jnp.where(keep, spread, 0.0), axis=2, keepdims=True).reshape(REQUESTS, 1)


def row_of(column):
    square = (REQUESTS, REQUESTS)
    spread = jnp.broadcast_to(column, square)
    return jnp.sum(jnp.where(iota(square, 0) == iota(square, 1), spread, 0.0), axis=0, keepdims=True)


def kernel(
    tokens_hbm, gain_ref, w_query_hbm, w_keyval_hbm, scale_ref, parents_ref, counts_ref,
    attended,
    tokens, w_query, w_keyval, normed, queries, keys, values, marks, summed, weighed, picked,
    ask, passed, asked, send, recv, place_of,
    load_sem, pass_send, pass_recv, ask_send, ask_recv, reply_send, reply_recv, self_sem,
):
    square = (REQUESTS, REQUESTS)
    loads = [
        pltpu.make_async_copy(source, target, load_sem.at[number])
        for number, (source, target) in enumerate(
            ((tokens_hbm, tokens), (w_keyval_hbm, w_keyval), (w_query_hbm, w_query))
        )
    ]
    for load in loads:
        load.start()

    barrier = pltpu.get_barrier_semaphore()

    row, col = lax.axis_index("row"), lax.axis_index("col")
    me = row * N_COL + col

    rows_at = [row_shifted(place) for place in range(N_ROW)]
    cols_at = [col_shifted(place, 1) for place in range(N_COL)]
    for place in range(1, N_ROW):
        pl.semaphore_signal(barrier, inc=1, device_id=(rows_at[place], col), device_id_type=MESH)
    for place in range(1, N_COL):
        pl.semaphore_signal(barrier, inc=1, device_id=(row, cols_at[place]), device_id_type=MESH)

    lane = iota(square, 1)
    lane_level, lane_slot, lane_child = lane // 8, lane // 4 % 2, lane % 4
    table = jnp.zeros(square, F32)
    for level in range(LEVELS):
        parent_col = column_of(parents_ref, level).astype(jnp.int32)
        parent_row = row_of(parent_col.astype(F32)).astype(jnp.int32)
        bits = 8 - 2 * level
        home_col, home_row = parent_col >> bits, parent_row >> bits
        local_row = (parent_row & ((1 << bits) - 1)).astype(F32)
        same = home_col == home_row
        rank_col = jnp.sum(ones_where(same & (iota(square, 1) < iota(square, 0))), axis=1, keepdims=True)
        rank_row = jnp.sum(ones_where(same & (iota(square, 0) < iota(square, 1))), axis=0, keepdims=True)
        place_of[level] = jnp.broadcast_to(home_col * 8 + rank_col.astype(jnp.int32) * 4, square)
        for slot in range(2):
            here = (iota(square, 0) == home_row) & (rank_row == float(slot))
            cell = jnp.sum(jnp.where(here, local_row, 0.0), axis=1, keepdims=True)
            table = jnp.where((lane_level == level) & (lane_slot == slot), cell, table)
    local = table.astype(jnp.int32)
    wide_bits = 4 - lane_level
    parent_r, parent_c = local >> wide_bits, local & ((1 << wide_bits) - 1)
    child = ((2 * parent_r + lane_child // 2) << (wide_bits + 1)) + 2 * parent_c + lane_child % 2
    ask[...] = child.reshape(DEVICES, 1, REQUESTS)

    own_pass = pltpu.make_async_copy(ask.at[pl.ds(row * N_COL, N_COL)], passed.at[row], self_sem.at[LEVELS])
    own_pass.start()
    pl.semaphore_wait(barrier, N_ROW + N_COL - 2)

    for place in range(1, N_ROW):
        pltpu.make_async_remote_copy(
            src_ref=ask.at[pl.ds(rows_at[place] * N_COL, N_COL)], dst_ref=passed.at[row], send_sem=pass_send,
            recv_sem=pass_recv, device_id=(rows_at[place], col), device_id_type=MESH,
        ).start()

    loads[0].wait()
    gain = gain_ref[...].reshape(1, WIDTH)

    def norm_rows(pair, carry):
        flat = tokens[pl.ds(2 * pair, 2)].reshape(2 * SIDE, WIDTH).astype(F32)
        centered = flat - jnp.mean(flat, axis=1, keepdims=True)
        spread = jnp.mean(centered * centered, axis=1, keepdims=True)
        result = centered * lax.rsqrt(spread + EPSILON) * gain
        tiled = result.reshape(2, 4, TILE, WIDTH).transpose(1, 0, 2, 3).reshape(4, 16, WIDTH).astype(BF16)
        for tile in range(4):
            start = pl.multiple_of((pair // 4 * 4 + tile) * OWN + pair % 4 * 16, 16)
            normed[pl.ds(start, 16), :] = tiled[tile]
        return carry

    lax.fori_loop(0, SIDE // 4, norm_rows, 0)
    own_pass.wait()
    pltpu.make_async_remote_copy(
        src_ref=passed.at[pl.ds(0, N_ROW - 1)], dst_ref=passed.at[pl.ds(0, N_ROW - 1)], send_sem=pass_send,
        recv_sem=pass_recv, device_id=(rows_at[1], col), device_id_type=MESH,
    ).wait()
    own_ask = pltpu.make_async_copy(passed.at[:, col], asked.at[0], self_sem.at[LEVELS])
    own_ask.start()

    for place in range(1, N_COL):
        to = col_shifted(place, -1)
        pltpu.make_async_remote_copy(
            src_ref=passed.at[:, to], dst_ref=asked.at[place], send_sem=ask_send, recv_sem=ask_recv,
            device_id=(row, to), device_id_type=MESH,
        ).start()

    lax.fori_loop(SIDE // 4, SIDE // 2, norm_rows, 0)

    own_ask.wait()
    pltpu.make_async_remote_copy(
        src_ref=asked.at[pl.ds(0, N_COL - 1)], dst_ref=asked.at[pl.ds(0, N_COL - 1)], send_sem=ask_send,
        recv_sem=ask_recv, device_id=(row, cols_at[1]), device_id_type=MESH,
    ).wait()
    token = iota((1, TOKENS), 1)
    token_r = token // 256 * 8 + token // 8 % 8
    token_c = token // 64 % 4 * 8 + token % 8
    place_in_eight = iota((SERVED, 8, REQUESTS), 1)
    lane_in_eight = iota((SERVED, 8, REQUESTS), 2)

    def gather(levels, block):
        first = pl.multiple_of(block * SERVED, SERVED)
        asks = asked[pl.ds(block * 4, 4)].astype(F32).reshape(SERVED, 1, REQUESTS)
        asks = jnp.broadcast_to(asks, (SERVED, 8, REQUESTS))
        picks = []
        for level in levels:
            cell_of = (token_r >> level) * (SIDE >> level) + (token_c >> level)
            wanted = jnp.where(lane_in_eight == place_in_eight + 8 * level, asks, 0.0)
            wanted = jnp.sum(wanted, axis=2, keepdims=True).reshape(SERVED * 8, 1).astype(jnp.int32)
            picks.append(jnp.where(wanted == cell_of, 0.25**level, 0.0).astype(BF16))
        pick = jnp.concatenate(picks, axis=0)
        left = dot(pick, normed[:, :HALF]).reshape(len(levels), SERVED, 8, HALF)
        right = dot(pick, normed[:, HALF:]).reshape(len(levels), SERVED, 8, HALF)
        for number, level in enumerate(levels):
            both = jnp.concatenate([left[number], right[number]], axis=1)
            send[level, pl.ds(first, SERVED)] = both.astype(BF16)

    def send_replies(level, blocks):
        for turn in range(SERVED * len(blocks)):
            block, off_z = blocks[turn // SERVED], turn % 4
            place = (turn // 4 + off_z) % 4 * 2 + turn % SERVED // 16
            if block == 0 and off_z == 0 and place == 0:
                continue
            pltpu.make_async_remote_copy(
                src_ref=send.at[level, block * SERVED + off_z * N_ROW + rows_at[place]],
                dst_ref=recv.at[level, me], send_sem=reply_send.at[level], recv_sem=reply_recv.at[level],
                device_id=(rows_at[place], cols_at[block * 4 + off_z]), device_id_type=MESH,
            ).start()

    def own_reply(level):
        return pltpu.make_async_copy(send.at[level, row], recv.at[level, me], self_sem.at[level])

    def gather_later(block, carry):
        gather((1, 2), block)
        return carry

    for block in range(DEVICES // SERVED):
        gather((0,), block)
        send_replies(0, (block,))
    lax.fori_loop(0, DEVICES // SERVED, gather_later, 0)
    send_replies(1, range(DEVICES // SERVED))
    for level in range(LEVELS):
        own_reply(level).start()

    block_ones = same_head()
    loads[1].wait()
    loads[2].wait()

    def project(block, carry):
        rows = pl.ds(pl.multiple_of(block * HALF, HALF), HALF)
        tiles = pl.ds(block * 8, 8)
        flat = normed[rows, :]
        for group in range(WIDTH // GROUP):
            span = slice(group * GROUP, (group + 1) * GROUP)
            scale = jnp.zeros((1, GROUP), F32)
            for head in range(4):
                scale = jnp.where(iota((1, GROUP), 1) // HEAD == head, scale_ref[group * 4 + head], scale)
            query = unit_heads(dot(flat, w_query[:, span]), block_ones) * scale
            queries[rows, span] = query.astype(BF16)
            key = dot(flat, w_keyval[:, span]).astype(BF16).astype(F32)
            keys[tiles, 0:OWN, span] = unit_heads(key, block_ones).astype(BF16).reshape(8, OWN, GROUP)
            value = dot(flat, w_keyval[:, WIDTH + group * GROUP : WIDTH + (group + 1) * GROUP])
            values[tiles, 0:OWN, span] = value.astype(BF16).reshape(8, OWN, GROUP)
        return carry

    lax.fori_loop(0, TOKENS // HALF, project, 0)
    marks[:, 0:OWN, :] = jnp.ones((TILES, OWN, REQUESTS), BF16)
    send_replies(2, range(DEVICES // SERVED))

    def by_tile(rows):
        columns = rows.shape[-1]
        return rows.reshape(4, TILES, TOPK, columns).transpose(1, 0, 2, 3).reshape(TILES, PER_LEVEL, columns)

    slots = iota((REQUESTS, DEVICES * 8), 1)
    early = OWN + (LEVELS - 1) * PER_LEVEL

    def sums_over(tile, group, first, last):
        masks = [ones_where(iota((last - first, GROUP), 1) // HEAD == head).astype(BF16) for head in range(4)]
        rows = pl.ds(pl.multiple_of(tile * OWN, OWN), OWN)
        span = slice(group * GROUP, (group + 1) * GROUP)
        key, value, mark = keys[tile, first:last, span], values[tile, first:last, span], marks[tile, first:last]
        mark = jnp.concatenate([mark, mark], axis=1)
        key, value, mark = [jnp.concatenate([part * mask for mask in masks], axis=0) for part in (key, value, mark)]
        weight = jnp.exp(dot_rows(queries[rows, span], key)).astype(BF16)
        return rows, span, dot(weight, value), dot(weight, mark)

    def own_keys(tile, carry):
        for group in range(WIDTH // GROUP):
            rows, span, top, bottom = sums_over(tile, group, 0, OWN)
            summed[rows, span] = top
            weighed[rows, span] = bottom
        return carry

    def early_keys(tile, carry):
        for group in range(WIDTH // GROUP):
            rows, span, top, bottom = sums_over(tile, group, OWN, early)
            summed[rows, span] += top
            weighed[rows, span] += bottom
        return carry

    lax.fori_loop(0, TILES, own_keys, 0, unroll=2)
    for level in range(LEVELS):
        if level == 2:
            lax.fori_loop(0, TILES, early_keys, 0, unroll=2)
        own_reply(level).wait()
        pltpu.make_async_remote_copy(
            src_ref=send.at[level, pl.ds(0, DEVICES - 1)], dst_ref=recv.at[level, pl.ds(0, DEVICES - 1)],
            send_sem=reply_send.at[level], recv_sem=reply_recv.at[level],
            device_id=(rows_at[1], col), device_id_type=MESH,
        ).wait()
        count_col = column_of(counts_ref, level)
        place_col = place_of[level][:, 0:1]
        valid = [count_col > float(child) for child in range(4)]
        marks[:, OWN + level * PER_LEVEL : OWN + (level + 1) * PER_LEVEL, :] = by_tile(
            jnp.concatenate([jnp.broadcast_to(ones_where(flag), square) for flag in valid], axis=0)
        ).astype(BF16)
        pick = jnp.concatenate(
            [ones_where((slots == place_col + child) & valid[child]).astype(BF16) for child in range(4)], axis=0
        )
        for side in range(2):
            rows = recv[level].astype(F32)[:, side * 8 : side * 8 + 8, :].reshape(DEVICES * 8, HALF).astype(BF16)
            picked[:, side * HALF : (side + 1) * HALF] = dot(pick, rows).astype(BF16)
        span_rows = slice(OWN + level * PER_LEVEL, OWN + (level + 1) * PER_LEVEL)
        for group in range(WIDTH // GROUP):
            span = slice(group * GROUP, (group + 1) * GROUP)
            key = dot(picked[...], w_keyval[:, span]).astype(BF16).astype(F32)
            keys[:, span_rows, span] = by_tile(unit_heads(key, block_ones)).astype(BF16)
            value = dot(picked[...], w_keyval[:, WIDTH + group * GROUP : WIDTH + (group + 1) * GROUP])
            values[:, span_rows, span] = by_tile(value).astype(BF16)

    def last_keys(tile, carry):
        for group in range(WIDTH // GROUP):
            rows, span, top, bottom = sums_over(tile, group, early, KEYS)
            attended[rows, span] = ((summed[rows, span] + top) / (weighed[rows, span] + bottom)).astype(BF16)
        return carry

    lax.fori_loop(0, TILES, last_keys, 0, unroll=2)


def mix(attended, w_output, out_ref):
    mixed = dot(attended[...], w_output[...]).reshape(4, TILE, TILE, WIDTH)
    out_ref[...] = mixed.transpose(1, 0, 2, 3).reshape(TILE, SIDE, WIDTH).astype(BF16)


def per_device(tokens, ln_gain, w_query, w_keyval, logit_scale, w_output, parents, child_counts):
    whole = pl.BlockSpec(memory_space=pltpu.VMEM)
    anywhere = pl.BlockSpec(memory_space=pl.ANY)
    attended = pl.pallas_call(
        kernel,
        out_shape=jax.ShapeDtypeStruct((TOKENS, WIDTH), BF16),
        in_specs=[anywhere, whole, anywhere, anywhere, pl.BlockSpec(memory_space=pltpu.SMEM), whole, whole],
        out_specs=whole,
        scratch_shapes=[
            pltpu.VMEM((SIDE, SIDE, WIDTH), BF16),
            pltpu.VMEM((WIDTH, WIDTH), BF16),
            pltpu.VMEM((WIDTH, 2 * WIDTH), BF16),
            pltpu.VMEM((TOKENS, WIDTH), BF16),
            pltpu.VMEM((TOKENS, WIDTH), BF16),
            pltpu.VMEM((TILES, KEYS, WIDTH), BF16),
            pltpu.VMEM((TILES, KEYS, WIDTH), BF16),
            pltpu.VMEM((TILES, KEYS, REQUESTS), BF16),
            pltpu.VMEM((TOKENS, WIDTH), F32),
            pltpu.VMEM((TOKENS, WIDTH), F32),
            pltpu.VMEM((4 * REQUESTS, WIDTH), BF16),
            pltpu.VMEM((DEVICES, 1, REQUESTS), jnp.int32),
            pltpu.VMEM((N_ROW, N_COL, 1, REQUESTS), jnp.int32),
            pltpu.VMEM((N_COL, N_ROW, 1, REQUESTS), jnp.int32),
            pltpu.VMEM((LEVELS, DEVICES, 16, HALF), BF16),
            pltpu.VMEM((LEVELS, DEVICES, 16, HALF), BF16),
            pltpu.VMEM((LEVELS, REQUESTS, REQUESTS), jnp.int32),
            pltpu.SemaphoreType.DMA((3,)),
            pltpu.SemaphoreType.DMA,
            pltpu.SemaphoreType.DMA,
            pltpu.SemaphoreType.DMA,
            pltpu.SemaphoreType.DMA,
            pltpu.SemaphoreType.DMA((LEVELS,)),
            pltpu.SemaphoreType.DMA((LEVELS,)),
            pltpu.SemaphoreType.DMA((LEVELS + 1,)),
        ],
        compiler_params=pltpu.CompilerParams(
            collective_id=0, has_side_effects=True, vmem_limit_bytes=60 * 2**20
        ),
    )(tokens, ln_gain, w_query, w_keyval, logit_scale, parents.transpose(0, 2, 1, 3), child_counts.transpose(0, 2, 1, 3))
    return pl.pallas_call(
        mix,
        grid=(TILES // 4,),
        out_shape=jax.ShapeDtypeStruct((SIDE, SIDE, WIDTH), BF16),
        in_specs=[
            pl.BlockSpec((4 * OWN, WIDTH), lambda block: (block, 0)),
            pl.BlockSpec((WIDTH, WIDTH), lambda block: (0, 0)),
        ],
        out_specs=pl.BlockSpec((TILE, SIDE, WIDTH), lambda block: (block, 0, 0)),
        compiler_params=pltpu.CompilerParams(vmem_limit_bytes=40 * 2**20),
    )(attended, w_output)


def solution(mesh):
    in_specs = (
        P("row", "col", None),
        P(),
        P(),
        P(),
        P(),
        P(),
        P("row", "col", None, None),
        P("row", "col", None, None),
    )
    return jax.shard_map(
        per_device, mesh=mesh, in_specs=in_specs, out_specs=P("row", "col", None), check_vma=False
    )
```

time: 129 us -> 115 us (0.89)
  Pallas kernels: 120 us -> 113 us
  local copies, waits for them, and re-layouts: 7.29 us -> 1.59 us
    pallas_call x1 -> x2, Pallas kernels: 120 us -> 113 us  [the longest x1 109 us: per_device(): pl.pallas_call(kernel, out_shape=jax.ShapeDtypeStruct((TOKENS, WIDTH), BF...]
    unnamed x3 -> x4, local copies, waits for them, and re-layouts: 5.89 us -> 1.59 us
where the time goes in v1:
time: 115 us
  Pallas kernels  113 us (98%)
  local copies, waits for them, and re-layouts  1.59 us (1%)
    pallas_call x1, Pallas kernels, per_device(): pl.pallas_call(kernel, out_shape=jax.ShapeDtypeStruct((TOKENS, WIDTH), BF...  109 us
    pallas_call x1, Pallas kernels, per_device(): pl.pallas_call(mix, grid=(TILES // 4,), out_shape=jax.ShapeDtypeStruct((S...  3.72 us

profile of v1, /device:TPU:9, one launch (start us, length us, event | category | flops | bytes accessed | tf_op | source)
XLA Modules:
  0.0 114.7 jit_solution(5189674690046312648)
XLA Ops:
  0.0 0.0 copy-start.1
  0.0 109.3 %shard_map.82.attended = bf16[1024,1024]{1,0:T(8,128)(2,1)} custom-call(bf16[32,32,1024]{2,1,0:T(8,128)(2,1)} %tokens_hbm.1, f32[1024]{0:T(1024)} %gain_ref.1, bf16[1024,1024]{1,0:T(8,128)(2,1)} %w_query_hbm.1, bf16[1024,2048]{1,0:T(8,128)(2,1)} %w_keyval_hbm.1, f32[16]{0:T(128)} %scale_ref.1, s32[4,3,4,8]{3,2,1,0:T(4,128)} %bitcast.2, s32[4,3,4,8]{3,2,1,0:T(4,128)} %bitcast.3), custom_call_target="tpu_custom_call" | custom-call | tf_op jit(solution)/shard_map/pallas_call | solution.py:347
  109.3 0.0 copy-done.1
  109.4 0.0 copy-start
  109.4 1.6 %copy-done = bf16[1024,1024]{1,0:T(8,128)(2,1)S(1)} copy-done((bf16[1024,1024]{1,0:T(8,128)(2,1)S(1)}, bf16[1024,1024]{1,0:T(8,128)(2,1)}, u32[]{:S(2)}) %copy-start) | copy-done | bytes 2097176
  110.9 3.7 %shard_map.83 = bf16[32,32,1024]{2,1,0:T(8,128)(2,1)} custom-call(bf16[1024,1024]{1,0:T(8,128)(2,1)S(1)} %copy-done, bf16[1024,1024]{1,0:T(8,128)(2,1)S(1)} %copy-done.1), custom_call_target="tpu_custom_call" | custom-call | tf_op jit(solution)/shard_map/pallas_call | solution.py:383
Async XLA Ops:
  0.0 109.3 %copy-start.1 = (bf16[1024,1024]{1,0:T(8,128)(2,1)S(1)}, bf16[1024,1024]{1,0:T(8,128)(2,1)}, u32[]{:S(2)}) copy-start(bf16[1024,1024]{1,0:T(8,128)(2,1)} %w_output.1) | copy-start | bytes 6291460
  109.4 1.6 %copy-start = (bf16[1024,1024]{1,0:T(8,128)(2,1)S(1)}, bf16[1024,1024]{1,0:T(8,128)(2,1)}, u32[]{:S(2)}) copy-start(bf16[1024,1024]{1,0:T(8,128)(2,1)} %shard_map.82.attended) | copy-start | bytes 6291460

commit v2 on v1

--- a/solution.py
+++ b/solution.py
@@ -226,6 +226,13 @@
                 device_id=(rows_at[place], cols_at[block * 4 + off_z]), device_id_type=MESH,
             ).start()
 
+    def all_replies(level):
+        return pltpu.make_async_remote_copy(
+            src_ref=send.at[level, pl.ds(0, DEVICES - 1)], dst_ref=recv.at[level, pl.ds(0, DEVICES - 1)],
+            send_sem=reply_send.at[level], recv_sem=reply_recv.at[level],
+            device_id=(rows_at[1], col), device_id_type=MESH,
+        )
+
     def own_reply(level):
         return pltpu.make_async_copy(send.at[level, row], recv.at[level, me], self_sem.at[level])
 
@@ -264,49 +271,45 @@
 
     lax.fori_loop(0, TOKENS // HALF, project, 0)
     marks[:, 0:OWN, :] = jnp.ones((TILES, OWN, REQUESTS), BF16)
-    send_replies(2, range(DEVICES // SERVED))
 
     def by_tile(rows):
         columns = rows.shape[-1]
         return rows.reshape(4, TILES, TOPK, columns).transpose(1, 0, 2, 3).reshape(TILES, PER_LEVEL, columns)
 
     slots = iota((REQUESTS, DEVICES * 8), 1)
-    early = OWN + (LEVELS - 1) * PER_LEVEL
-
-    def sums_over(tile, group, first, last):
-        masks = [ones_where(iota((last - first, GROUP), 1) // HEAD == head).astype(BF16) for head in range(4)]
+    early = OWN + PER_LEVEL
+
+    def head_masks(count):
+        return [ones_where(iota((count, GROUP), 1) // HEAD == head).astype(BF16) for head in range(4)]
+
+    def marks_over(tile, first, last):
+        mark = marks[tile, first:last]
+        mark = jnp.concatenate([mark, mark], axis=1)
+        return jnp.concatenate([mark * mask for mask in head_masks(last - first)], axis=0)
+
+    def sums_over(tile, group, mark, first, last):
+        masks = head_masks(last - first)
         rows = pl.ds(pl.multiple_of(tile * OWN, OWN), OWN)
         span = slice(group * GROUP, (group + 1) * GROUP)
-        key, value, mark = keys[tile, first:last, span], values[tile, first:last, span], marks[tile, first:last]
-        mark = jnp.concatenate([mark, mark], axis=1)
-        key, value, mark = [jnp.concatenate([part * mask for mask in masks], axis=0) for part in (key, value, mark)]
+        key = jnp.concatenate([keys[tile, first:last, span] * mask for mask in masks], axis=0)
+        value = jnp.concatenate([values[tile, first:last, span] * mask for mask in masks], axis=0)
         weight = jnp.exp(dot_rows(queries[rows, span], key)).astype(BF16)
         return rows, span, dot(weight, value), dot(weight, mark)
 
-    def own_keys(tile, carry):
+    def early_keys(tile, carry):
+        mark = marks_over(tile, 0, early)
         for group in range(WIDTH // GROUP):
-            rows, span, top, bottom = sums_over(tile, group, 0, OWN)
+            rows, span, top, bottom = sums_over(tile, group, mark, 0, early)
             summed[rows, span] = top
             weighed[rows, span] = bottom
         return carry
 
-    def early_keys(tile, carry):
-        for group in range(WIDTH // GROUP):
-            rows, span, top, bottom = sums_over(tile, group, OWN, early)
-            summed[rows, span] += top
-            weighed[rows, span] += bottom
-        return carry
-
-    lax.fori_loop(0, TILES, own_keys, 0, unroll=2)
+    send_replies(2, range(DEVICES // SERVED))
     for level in range(LEVELS):
-        if level == 2:
+        if level == 1:
             lax.fori_loop(0, TILES, early_keys, 0, unroll=2)
         own_reply(level).wait()
-        pltpu.make_async_remote_copy(
-            src_ref=send.at[level, pl.ds(0, DEVICES - 1)], dst_ref=recv.at[level, pl.ds(0, DEVICES - 1)],
-            send_sem=reply_send.at[level], recv_sem=reply_recv.at[level],
-            device_id=(rows_at[1], col), device_id_type=MESH,
-        ).wait()
+        all_replies(level).wait()
         count_col = column_of(counts_ref, level)
         place_col = place_of[level][:, 0:1]
         valid = [count_col > float(child) for child in range(4)]
@@ -328,17 +331,30 @@
             values[:, span_rows, span] = by_tile(value).astype(BF16)
 
     def last_keys(tile, carry):
+        mark = marks_over(tile, early, KEYS)
         for group in range(WIDTH // GROUP):
-            rows, span, top, bottom = sums_over(tile, group, early, KEYS)
+            rows, span, top, bottom = sums_over(tile, group, mark, early, KEYS)
             attended[rows, span] = ((summed[rows, span] + top) / (weighed[rows, span] + bottom)).astype(BF16)
         return carry
 
-    lax.fori_loop(0, TILES, last_keys, 0, unroll=2)
-
-
-def mix(attended, w_output, out_ref):
-    mixed = dot(attended[...], w_output[...]).reshape(4, TILE, TILE, WIDTH)
-    out_ref[...] = mixed.transpose(1, 0, 2, 3).reshape(TILE, SIDE, WIDTH).astype(BF16)
+    lax.fori_loop(0, TILES, last_keys, 0, unroll=4)
+
+
+def mix(attended, w_output, out_hbm, mixed, store_sem):
+    blocks = TILES // 4
+    stores = [
+        pltpu.make_async_copy(
+            mixed.at[pl.ds(block * TILE, TILE)], out_hbm.at[pl.ds(block * TILE, TILE)], store_sem.at[block]
+        )
+        for block in range(blocks)
+    ]
+    for block in range(blocks):
+        result = dot(attended[block * GROUP : (block + 1) * GROUP], w_output[...]).reshape(4, TILE, TILE, WIDTH)
+        result = result.transpose(1, 0, 2, 3).reshape(TILE, SIDE, WIDTH)
+        mixed[block * TILE : (block + 1) * TILE] = result.astype(BF16)
+        stores[block].start()
+    for store in stores:
+        store.wait()
 
 
 def per_device(tokens, ln_gain, w_query, w_keyval, logit_scale, w_output, parents, child_counts):
@@ -382,14 +398,14 @@
     )(tokens, ln_gain, w_query, w_keyval, logit_scale, parents.transpose(0, 2, 1, 3), child_counts.transpose(0, 2, 1, 3))
     return pl.pallas_call(
         mix,
-        grid=(TILES // 4,),
         out_shape=jax.ShapeDtypeStruct((SIDE, SIDE, WIDTH), BF16),
-        in_specs=[
-            pl.BlockSpec((4 * OWN, WIDTH), lambda block: (block, 0)),
-            pl.BlockSpec((WIDTH, WIDTH), lambda block: (0, 0)),
+        in_specs=[whole, whole],
+        out_specs=pl.BlockSpec(memory_space=pltpu.HBM),
+        scratch_shapes=[
+            pltpu.VMEM((SIDE, SIDE, WIDTH), BF16),
+            pltpu.SemaphoreType.DMA((TILES // 4,)),
         ],
-        out_specs=pl.BlockSpec((TILE, SIDE, WIDTH), lambda block: (block, 0, 0)),
-        compiler_params=pltpu.CompilerParams(vmem_limit_bytes=40 * 2**20),
+        compiler_params=pltpu.CompilerParams(vmem_limit_bytes=24 * 2**20),
     )(attended, w_output)
 
 

time: 115 us -> 109 us (0.948)
  Pallas kernels: 113 us -> 107 us
    pallas_call x1, Pallas kernels: 109 us -> 104 us  [per_device(): pl.pallas_call(kernel, out_shape=jax.ShapeDtypeStruct((TOKENS, WIDTH), BF...]
where the time goes in v2:
time: 109 us
  Pallas kernels  107 us (98%)
  local copies, waits for them, and re-layouts  1.59 us (1%)
    pallas_call x1, Pallas kernels, per_device(): pl.pallas_call(kernel, out_shape=jax.ShapeDtypeStruct((TOKENS, WIDTH), BF...  104 us
    pallas_call x1, Pallas kernels, per_device(): pl.pallas_call(mix, out_shape=jax.ShapeDtypeStruct((SIDE, SIDE, WIDTH), B...  3.16 us

profile of v2, /device:TPU:9, one launch (start us, length us, event | category | flops | bytes accessed | tf_op | source)
XLA Modules:
  0.0 108.5 jit_solution(2257293854432776434)
XLA Ops:
  0.0 0.0 copy-start.1
  0.0 103.6 %shard_map.82.attended = bf16[1024,1024]{1,0:T(8,128)(2,1)} custom-call(bf16[32,32,1024]{2,1,0:T(8,128)(2,1)} %tokens_hbm.1, f32[1024]{0:T(1024)} %gain_ref.1, bf16[1024,1024]{1,0:T(8,128)(2,1)} %w_query_hbm.1, bf16[1024,2048]{1,0:T(8,128)(2,1)} %w_keyval_hbm.1, f32[16]{0:T(128)} %scale_ref.1, s32[4,3,4,8]{3,2,1,0:T(4,128)} %bitcast.2, s32[4,3,4,8]{3,2,1,0:T(4,128)} %bitcast.3), custom_call_target="tpu_custom_call" | custom-call | tf_op jit(solution)/shard_map/pallas_call | solution.py:363
  103.6 0.0 copy-done.1
  103.6 0.0 copy-start
  103.6 1.6 %copy-done = bf16[1024,1024]{1,0:T(8,128)(2,1)S(1)} copy-done((bf16[1024,1024]{1,0:T(8,128)(2,1)S(1)}, bf16[1024,1024]{1,0:T(8,128)(2,1)}, u32[]{:S(2)}) %copy-start) | copy-done | bytes 2097176
  105.2 3.2 %shard_map.83 = bf16[32,32,1024]{2,1,0:T(8,128)(2,1)} custom-call(bf16[1024,1024]{1,0:T(8,128)(2,1)S(1)} %copy-done, bf16[1024,1024]{1,0:T(8,128)(2,1)S(1)} %copy-done.1), custom_call_target="tpu_custom_call" | custom-call | tf_op jit(solution)/shard_map/pallas_call | solution.py:399
Async XLA Ops:
  0.0 103.6 %copy-start.1 = (bf16[1024,1024]{1,0:T(8,128)(2,1)S(1)}, bf16[1024,1024]{1,0:T(8,128)(2,1)}, u32[]{:S(2)}) copy-start(bf16[1024,1024]{1,0:T(8,128)(2,1)} %w_output.1) | copy-start | bytes 6291460
  103.6 1.6 %copy-start = (bf16[1024,1024]{1,0:T(8,128)(2,1)S(1)}, bf16[1024,1024]{1,0:T(8,128)(2,1)}, u32[]{:S(2)}) copy-start(bf16[1024,1024]{1,0:T(8,128)(2,1)} %shard_map.82.attended) | copy-start | bytes 6291460

commit v3 on v2

--- a/solution.py
+++ b/solution.py
@@ -287,19 +287,23 @@
         mark = jnp.concatenate([mark, mark], axis=1)
         return jnp.concatenate([mark * mask for mask in head_masks(last - first)], axis=0)
 
-    def sums_over(tile, group, mark, first, last):
+    def sums_over(tile, first, last):
         masks = head_masks(last - first)
         rows = pl.ds(pl.multiple_of(tile * OWN, OWN), OWN)
-        span = slice(group * GROUP, (group + 1) * GROUP)
-        key = jnp.concatenate([keys[tile, first:last, span] * mask for mask in masks], axis=0)
-        value = jnp.concatenate([values[tile, first:last, span] * mask for mask in masks], axis=0)
-        weight = jnp.exp(dot_rows(queries[rows, span], key)).astype(BF16)
-        return rows, span, dot(weight, value), dot(weight, mark)
+        weights, tops = [], []
+        for group in range(WIDTH // GROUP):
+            span = slice(group * GROUP, (group + 1) * GROUP)
+            key = jnp.concatenate([keys[tile, first:last, span] * mask for mask in masks], axis=0)
+            value = jnp.concatenate([values[tile, first:last, span] * mask for mask in masks], axis=0)
+            weights.append(jnp.exp(dot_rows(queries[rows, span], key)).astype(BF16))
+            tops.append(dot(weights[group], value))
+        bottoms = dot(jnp.concatenate(weights, axis=0), marks_over(tile, first, last))
+        for group in range(WIDTH // GROUP):
+            span = slice(group * GROUP, (group + 1) * GROUP)
+            yield rows, span, tops[group], bottoms[group * OWN : (group + 1) * OWN]
 
     def early_keys(tile, carry):
-        mark = marks_over(tile, 0, early)
-        for group in range(WIDTH // GROUP):
-            rows, span, top, bottom = sums_over(tile, group, mark, 0, early)
+        for rows, span, top, bottom in sums_over(tile, 0, early):
             summed[rows, span] = top
             weighed[rows, span] = bottom
         return carry
@@ -331,9 +335,7 @@
             values[:, span_rows, span] = by_tile(value).astype(BF16)
 
     def last_keys(tile, carry):
-        mark = marks_over(tile, early, KEYS)
-        for group in range(WIDTH // GROUP):
-            rows, span, top, bottom = sums_over(tile, group, mark, early, KEYS)
+        for rows, span, top, bottom in sums_over(tile, early, KEYS):
             attended[rows, span] = ((summed[rows, span] + top) / (weighed[rows, span] + bottom)).astype(BF16)
         return carry
 

time: 109 us -> 113 us (1.037)
  Pallas kernels: 107 us -> 111 us
    pallas_call x1, Pallas kernels: 104 us -> 108 us  [per_device(): pl.pallas_call(kernel, out_shape=jax.ShapeDtypeStruct((TOKENS, WIDTH), BF...]
where the time goes in v3:
time: 113 us
  Pallas kernels  111 us (98%)
  local copies, waits for them, and re-layouts  1.59 us (1%)
    pallas_call x1, Pallas kernels, per_device(): pl.pallas_call(kernel, out_shape=jax.ShapeDtypeStruct((TOKENS, WIDTH), BF...  108 us
    pallas_call x1, Pallas kernels, per_device(): pl.pallas_call(mix, out_shape=jax.ShapeDtypeStruct((SIDE, SIDE, WIDTH), B...  3.16 us

profile of v3, /device:TPU:9, one launch (start us, length us, event | category | flops | bytes accessed | tf_op | source)
XLA Modules:
  0.0 113.3 jit_solution(8399621279162359549)
XLA Ops:
  0.0 0.0 copy-start.1
  0.0 108.3 %shard_map.82.attended = bf16[1024,1024]{1,0:T(8,128)(2,1)} custom-call(bf16[32,32,1024]{2,1,0:T(8,128)(2,1)} %tokens_hbm.1, f32[1024]{0:T(1024)} %gain_ref.1, bf16[1024,1024]{1,0:T(8,128)(2,1)} %w_query_hbm.1, bf16[1024,2048]{1,0:T(8,128)(2,1)} %w_keyval_hbm.1, f32[16]{0:T(128)} %scale_ref.1, s32[4,3,4,8]{3,2,1,0:T(4,128)} %bitcast.2, s32[4,3,4,8]{3,2,1,0:T(4,128)} %bitcast.3), custom_call_target="tpu_custom_call" | custom-call | tf_op jit(solution)/shard_map/pallas_call | solution.py:365
  108.3 0.0 copy-done.1
  108.3 0.0 copy-start
  108.4 1.6 %copy-done = bf16[1024,1024]{1,0:T(8,128)(2,1)S(1)} copy-done((bf16[1024,1024]{1,0:T(8,128)(2,1)S(1)}, bf16[1024,1024]{1,0:T(8,128)(2,1)}, u32[]{:S(2)}) %copy-start) | copy-done | bytes 2097176
  109.9 3.2 %shard_map.83 = bf16[32,32,1024]{2,1,0:T(8,128)(2,1)} custom-call(bf16[1024,1024]{1,0:T(8,128)(2,1)S(1)} %copy-done, bf16[1024,1024]{1,0:T(8,128)(2,1)S(1)} %copy-done.1), custom_call_target="tpu_custom_call" | custom-call | tf_op jit(solution)/shard_map/pallas_call | solution.py:401
Async XLA Ops:
  0.0 108.3 %copy-start.1 = (bf16[1024,1024]{1,0:T(8,128)(2,1)S(1)}, bf16[1024,1024]{1,0:T(8,128)(2,1)}, u32[]{:S(2)}) copy-start(bf16[1024,1024]{1,0:T(8,128)(2,1)} %w_output.1) | copy-start | bytes 6291460
  108.3 1.6 %copy-start = (bf16[1024,1024]{1,0:T(8,128)(2,1)S(1)}, bf16[1024,1024]{1,0:T(8,128)(2,1)}, u32[]{:S(2)}) copy-start(bf16[1024,1024]{1,0:T(8,128)(2,1)} %shard_map.82.attended) | copy-start | bytes 6291460
